TPU v7x, 256 devices: a whole 4x4x8 slice. The times are simulated.
256 devices in a mesh: dp: 4 (over x), seq: 32 (over z, y), head: 2 (over core).
Axes of the slice: x: 4, y: 4, z: 8, core: 2. Of those that a mesh axis runs over, the one named last changes fastest.
Arguments:
- queries: bfloat16 [32768, 1536], P(('dp', 'seq'), 'head'), parts along dimension 0, may hold values from -8 to 8
- keys: bfloat16 [32768, 1536], P(('dp', 'seq'), 'head'), parts along dimension 0, may hold values from -8 to 8
- values: bfloat16 [32768, 1536], P(('dp', 'seq'), 'head'), parts along dimension 0, may hold values from -18 to 18
- tile_lists: int32 [128, 8], replicated, may hold values from 0 to 127, as said below
- out_weight: bfloat16 [1536, 3072], P('head'), may hold values from -0.15625 to 0.15625
Outputs:
- mixed: bfloat16 [32768, 3072], P(('dp', 'seq', 'head')), parts along dimension 0
There are 4 independent parts, one for each index of `dp`. A program takes and returns all parts, laid end to end along the dimension named above; an argument that names none is the same for every part. Nothing has to cross between parts.
Inputs may be any that keep to these rules, and one draw needn't show every extreme that they name: `tile_lists`: tiles come in frames of 4 consecutive tiles (a 2 x 2 grid of rows and columns). Each row lists the 8 tiles of two consecutive frames, one of which is the query tile's frame; so the query tile itself is always listed, and a listed tile's frame differs from the query tile's by at most one.
All inputs are finite; a program needn't handle non-finite values.
Results may differ from a plain program's by a relative error of at most 0.015.
Values may be sent and summed in bfloat16 or wider, within the bound.
A program may use at most 64 MiB of HBM per device.

v0:
```python
import jax
import jax.numpy as jnp
from jax import lax
from jax.sharding import PartitionSpec as P

HD = 128
TILES_DEV = 4


NEGATIVE = -1e30


def from_behind(value, axis, steps):
    count = lax.axis_size(axis)
    leading, last = (max(0, -steps), min(count, count - steps))
    return lax.ppermute(value, axis, [(source, source + steps) for source in range(leading, last)])


def tile_allowed(tile_lists, owner_index, holder, tile_rows):
    listed = lax.dynamic_slice_in_dim(tile_lists, owner_index * TILES_DEV, TILES_DEV, 0)
    held_ids = holder * TILES_DEV + jnp.arange(TILES_DEV, dtype=jnp.int32)
    matched = jnp.any(listed[:, :, None] == held_ids[None, None, :], axis=1)
    spread = jnp.broadcast_to(
        matched[:, None, :, None], (TILES_DEV, tile_rows, TILES_DEV, tile_rows)
    )
    return spread.reshape(TILES_DEV * tile_rows, TILES_DEV * tile_rows)


def block_partial(query_block, stacked, allowed):
    score_scale = query_block.shape[-1] ** (-0.5)
    scores = (
        jnp.einsum("qhd,khd->qhk", query_block, stacked[0], preferred_element_type=jnp.float32)
        * score_scale
    )
    allowed_three = allowed[:, None, :]
    scores = jnp.where(allowed_three, scores, NEGATIVE)
    maximum = jnp.max(scores, axis=-1)
    weights = jnp.where(allowed_three, jnp.exp(scores - maximum[..., None]), 0.0)
    denominator = jnp.sum(weights, axis=-1)
    summed = jnp.einsum(
        "qhk,khd->qhd", weights.astype(jnp.bfloat16), stacked[1], preferred_element_type=jnp.float32
    )
    maximum = jnp.where(denominator > 0, maximum, NEGATIVE)
    return (summed, maximum, denominator)


def combine(earlier_part, later_part):
    summed_one, maximum_one, denominator_one = earlier_part
    summed_two, maximum_two, denominator_two = later_part
    maximum_one = jnp.where(denominator_one > 0, maximum_one, NEGATIVE)
    maximum_two = jnp.where(denominator_two > 0, maximum_two, NEGATIVE)
    joined = jnp.maximum(maximum_one, maximum_two)
    factor_one = jnp.exp(maximum_one - joined)
    factor_two = jnp.exp(maximum_two - joined)
    summed = summed_one * factor_one[..., None] + summed_two * factor_two[..., None]
    return (summed, joined, denominator_one * factor_one + denominator_two * factor_two)


def on_device(queries, keys, values, tile_lists, out_weight):
    token_count = queries.shape[0]
    columns = queries.shape[1]
    groups = columns // HD
    tile_rows = token_count // TILES_DEV
    local_queries = queries.reshape(token_count, groups, HD)
    stacked = jnp.stack([keys, values]).reshape(2, token_count, groups, HD)
    position = lax.axis_index("seq")
    running = block_partial(
        local_queries, stacked, tile_allowed(tile_lists, position, position, tile_rows)
    )
    from_before = from_behind(stacked, "seq", 1)
    from_after = from_behind(stacked, "seq", -1)
    running = combine(
        running,
        block_partial(
            local_queries, from_before, tile_allowed(tile_lists, position, position - 1, tile_rows)
        ),
    )
    running = combine(
        running,
        block_partial(
            local_queries, from_after, tile_allowed(tile_lists, position, position + 1, tile_rows)
        ),
    )
    summed, maximum, denominator = running
    attended = (summed / denominator[..., None]).astype(jnp.bfloat16).reshape(token_count, columns)
    return lax.psum_scatter(
        jnp.dot(attended, out_weight, preferred_element_type=jnp.float32).astype(jnp.bfloat16),
        "head",
        scatter_dimension=0,
        tiled=True,
    )


def solution(mesh):
    placed = (
        P(("dp", "seq"), "head"),
        P(("dp", "seq"), "head"),
        P(("dp", "seq"), "head"),
        P(),
        P("head", None),
    )
    return jax.shard_map(
        on_device,
        mesh=mesh,
        in_specs=placed,
        out_specs=P(("dp", "seq", "head"), None),
        check_vma=False,
    )
```

profile of v0, /device:TPU:1, one launch (start us, length us, event | category | flops | bytes accessed | tf_op | source)
XLA Modules:
  0.0 72.4 jit_solution(18079789832064179138)
XLA Ops:
  6.5 1.2 %copy.36 = bf16[256,768]{0,1:T(8,128)(2,1)S(1)} copy(bf16[256,768]{1,0:T(8,128)(2,1)} %param.6) | data formatting | bytes 786432 | tf_op args[1]
  7.7 1.2 %copy.40 = bf16[256,768]{0,1:T(8,128)(2,1)S(1)} copy(bf16[256,768]{1,0:T(8,128)(2,1)} %param.7) | data formatting | bytes 786432 | tf_op args[2]
  8.9 0.2 copy.46
  9.1 0.2 copy.45
  9.4 1.0 %pad_maximum_fusion = bf16[2,256,6,128]{3,1,2,0:T(8,128)(2,1)} fusion(bf16[1,256,6,128]{3,1,2,0:T(8,128)(2,1)S(1)} %copy.46, bf16[1,256,6,128]{3,1,2,0:T(8,128)(2,1)S(1)} %copy.45), kind=kLoop, calls=%fused_computation.24 | loop fusion | flops 393216 | bytes 1572864 | tf_op jit(solution)/shard_map/stack | solution.py:65
  10.3 1.3 %collective-permute-start.1 = (bf16[2,256,6,128]{3,1,2,0:T(8,128)(2,1)}, bf16[2,256,6,128]{3,1,2,0:T(8,128)(2,1)}, u32[]{:S(2)}, u32[]{:S(2)}) collective-permute-start(bf16[2,256,6,128]{3,1,2,0:T(8,128)(2,1)} %pad_maximum_fusion), channel_id=1, source_target_pairs={{2,0},{4,2},{6,4},{8,6},{10,8},{12,10},{14,12},{16,14},{18,16},{20... | collective-permute-start | bytes 2359304 | tf_op jit(solution)/shard_map/ppermute | solution.py:16
  11.6 5.6 %collective-permute-start = (bf16[2,256,6,128]{3,1,2,0:T(8,128)(2,1)}, bf16[2,256,6,128]{3,1,2,0:T(8,128)(2,1)}, u32[]{:S(2)}, u32[]{:S(2)}) collective-permute-start(bf16[2,256,6,128]{3,1,2,0:T(8,128)(2,1)} %pad_maximum_fusion), channel_id=1, source_target_pairs={{0,2},{2,4},{4,6},{6,8},{8,10},{10,12},{12,14},{14,16},{16,18},{18... | collective-permute-start | bytes 2359304 | tf_op jit(solution)/shard_map/ppermute | solution.py:16
  17.4 0.4 compare_reduce_fusion.2
  18.0 0.2 broadcast_in_dim.87
  18.2 0.2 copy.37
  18.4 0.5 fusion.33
  19.2 0.2 broadcast_in_dim.96
  19.6 0.2 broadcast_in_dim.93
  19.9 0.3 fusion.7
  20.2 10.4 %collective-permute-done = bf16[2,256,6,128]{3,1,2,0:T(8,128)(2,1)} collective-permute-done((bf16[2,256,6,128]{3,1,2,0:T(8,128)(2,1)}, bf16[2,256,6,128]{3,1,2,0:T(8,128)(2,1)}, u32[]{:S(2)}, u32[]{:S(2)}) %collective-permute-start) | collective-permute-done | bytes 786464 | tf_op jit(solution)/shard_map/ppermute | solution.py:16
  30.6 1.4 %fusion.32 = (f32[256,6]{0,1:T(8,128)S(1)}, f32[256,6,256]{0,2,1:T(8,128)S(1)}) fusion(bf16[256,6,128]{0,2,1:T(8,128)(2,1)S(1)} %bitcast.66, bf16[2,256,6,128]{3,1,2,0:T(8,128)(2,1)} %collective-permute-done, pred[256,256]{0,1:T(8,128)(4,1)S(1)} %broadcast_in_dim.93), kind=kOutput, calls=%fused_computation.61 | convolution fusion | flops 101841408 | bytes 2430976 | tf_op jit(solution)/shard_map/qhd,khd->qhk/dot_general | solution.py:32
  32.0 0.3 fusion.10
  32.3 1.4 %fusion.31 = (f32[256,6]{0,1:T(8,128)S(1)}, f32[256,6,256]{0,2,1:T(8,128)S(1)}) fusion(bf16[256,6,128]{0,2,1:T(8,128)(2,1)S(1)} %bitcast.67, bf16[2,256,6,128]{3,1,2,0:T(8,128)(2,1)} %collective-permute-done.1, pred[256,256]{0,1:T(8,128)(4,1)S(1)} %broadcast_in_dim.96), kind=kOutput, calls=%fused_computation.60 | convolution fusion | flops 101841408 | bytes 2430976 | tf_op jit(solution)/shard_map/qhd,khd->qhk/dot_general | solution.py:32
  33.7 0.3 fusion.12
  34.0 0.4 fusion.6
  34.4 1.8 %fusion.5 = f32[256,6,128]{0,2,1:T(8,128)S(1)} fusion(f32[256,6,256]{0,2,1:T(8,128)S(1)} %get-tuple-element.14, f32[256,6]{0,1:T(8,128)S(1)} %get-tuple-element.13, pred[256,256]{0,1:T(8,128)(4,1)S(1)} %broadcast_in_dim.96, bf16[2,256,6,128]{3,1,2,0:T(8,128)(2,1)} %collective-permute-done.1, f32[256,6]{0,1:T(8,128)S(1)} %get-tuple-element.10), kind=kOutput, calls=%fused_computation.15 | convolution fusion | flops 102039552 | bytes 2830336 | tf_op jit(solution)/shard_map/qhk,khd->qhd/dot_general | solution.py:40
  36.3 1.5 %fusion.13 = bf16[256,6,128]{0,2,1:T(8,128)(2,1)S(1)} fusion(f32[256,6,128]{0,2,1:T(8,128)S(1)} %fusion.5, f32[256,6,128]{0,2,1:T(8,128)S(1)} %fusion.6, f32[256,6,256]{0,2,1:T(8,128)S(1)} %get-tuple-element.16, f32[256,6]{0,1:T(8,128)S(1)} %get-tuple-element.15, pred[256,256]{0,1:T(8,128)(4,1)S(1)} %broadcast_in_dim.93, ...), kind=kOutput, calls=%fused_computation.23 | convolution fusion | flops 103022592 | bytes 4022272 | tf_op jit(solution)/shard_map/qhk,khd->qhd/dot_general | solution.py:40
  37.8 2.6 %convolution_convert_fusion = bf16[256,3072]{1,0:T(8,128)(2,1)} fusion(bf16[256,768]{0,1:T(8,128)(2,1)S(1)} %bitcast.72, bf16[768,3072]{1,0:T(8,128)(2,1)S(1)} %bitcast.64), kind=kOutput, calls=%fused_computation | convolution fusion | flops 1208745984 | bytes 6684672 | tf_op jit(solution)/shard_map/dot_general | solution.py:87
  40.4 25.1 %reduce-scatter.2.cloned.1.call-done = bf16[128,3072]{1,0:T(8,128)(2,1)} async-done(((bf16[256,3072]{1,0:T(8,128)(2,1)}), bf16[128,3072]{1,0:T(8,128)(2,1)}) %reduce-scatter.2.cloned.1.call-update) | async-done | bytes 786448 | tf_op jit(solution)/shard_map/reduce_scatter | solution.py:86
  (23 shorter events, 1.0 us)
Async XLA Ops:
  6.5 10.7 %copy-start = (s32[128,8]{0,1:T(8,128)S(1)}, s32[128,8]{0,1:T(8,128)}, u32[]{:S(2)}) copy-start(s32[128,8]{0,1:T(8,128)} %param.8) | copy-start | bytes 12292
  6.5 59.0 %reduce-scatter.2.cloned.1.call-start = ((), (), s32[]{:S(2)}) async-start(), calls=%async_computation.1 | async-start | bytes 2359296 | tf_op jit(solution)/shard_map/reduce_scatter | solution.py:86
  8.9 9.4 %copy-start.1 = (bf16[256,768]{1,0:T(8,128)(2,1)S(1)}, bf16[256,768]{1,0:T(8,128)(2,1)}, u32[]{:S(2)}) copy-start(bf16[256,768]{1,0:T(8,128)(2,1)} %param.5) | copy-start | bytes 1179652
  10.3 21.9 %collective-permute-start.1 = (bf16[2,256,6,128]{3,1,2,0:T(8,128)(2,1)}, bf16[2,256,6,128]{3,1,2,0:T(8,128)(2,1)}, u32[]{:S(2)}, u32[]{:S(2)}) collective-permute-start(bf16[2,256,6,128]{3,1,2,0:T(8,128)(2,1)} %pad_maximum_fusion), channel_id=1, source_target_pairs={{2,0},{4,2},{6,4},{8,6},{10,8},{12,10},{14,12},{16,14},{18,16},{20... | collective-permute-start | bytes 2359304 | tf_op jit(solution)/shard_map/ppermute | solution.py:16
  11.6 18.9 %collective-permute-start = (bf16[2,256,6,128]{3,1,2,0:T(8,128)(2,1)}, bf16[2,256,6,128]{3,1,2,0:T(8,128)(2,1)}, u32[]{:S(2)}, u32[]{:S(2)}) collective-permute-start(bf16[2,256,6,128]{3,1,2,0:T(8,128)(2,1)} %pad_maximum_fusion), channel_id=1, source_target_pairs={{0,2},{2,4},{4,6},{6,8},{8,10},{10,12},{12,14},{14,16},{16,18},{18... | collective-permute-start | bytes 2359304 | tf_op jit(solution)/shard_map/ppermute | solution.py:16
  33.7 4.1 %slice-start = ((s8[4718592]{0:T(1024)(128)(4,1)}), s8[4194304]{0:T(1024)(128)(4,1)S(1)}, s32[]{:S(2)}) async-start(s8[4718592]{0:T(1024)(128)(4,1)} %bitcast.63), calls=%async_computation.2 | async-start | bytes 8388608
  34.4 3.3 %slice-start.1 = ((s8[4718592]{0:T(1024)(128)(4,1)}), s8[524288]{0:T(1024)(128)(4,1)S(1)}, s32[]{:S(2)}) async-start(s8[4718592]{0:T(1024)(128)(4,1)} %bitcast.63), calls=%async_computation.3 | async-start | bytes 1048576
Sparse Core Ops, SparseCore 0:
  40.5 24.9 reduce-scatter.1
where the time goes:
time: 72.7 us; the launch traced here: 72.4 us
  waiting for transfers between devices  35.6 us (49%)
  between operations  13.6 us (19%)
  matrix products  9.52 us (13%)
  starting transfers between devices  6.86 us (9%)
  local copies, waits for them, and re-layouts  4.65 us (6%)
  other arithmetic  2.21 us (3%)
    reduce_scatter x1, waiting for transfers between devices, on_device(): lax.psum_scatter(jnp.dot(attended, out_weight, preferred_element_type=jnp...  25.1 us
    ppermute x2, waiting for transfers between devices, from_behind(): lax.ppermute(value, axis, [(source, source + steps) for source in range(l...  10.4 us
    ppermute x2, starting transfers between devices, from_behind(): lax.ppermute(value, axis, [(source, source + steps) for source in range(l...  6.85 us
    dot_general x3, matrix products, block_partial(): jnp.einsum('qhk,khd->qhd', weights.astype(jnp.bfloat16), stacked[1], pref...  3.7 us
    dot_general x3, matrix products, block_partial(): jnp.einsum('qhd,khd->qhk', query_block, stacked[0], preferred_element_typ...  3.21 us
    dot_general x1, matrix products, on_device(): jnp.dot(attended, out_weight, preferred_element_type=jnp.float32)  2.61 us
    unnamed x11, local copies, waits for them, and re-layouts  2.54 us
  transfers between devices with their start and end apart: 3, of which 2 were waited for; matrix products, arithmetic and copies ran while one was open for 6% of the time, Pallas kernels for 0%

commit v1 on v0

v1 whole, which is shorter than its diff:
```python
import functools

import jax
import jax.numpy as jnp
from jax import lax
from jax.experimental import pallas as pl
from jax.experimental.pallas import tpu as pltpu
from jax.sharding import PartitionSpec as P

HD = 128
TILES_DEV = 4
MESH = pl.DeviceIdType.MESH
OWN, BEFORE, AFTER = 0, 1, 2
K, V = 0, 1


def remote(src, dst, send_sem, recv_sem, device):
    return pltpu.make_async_remote_copy(
        src_ref=src,
        dst_ref=dst,
        send_sem=send_sem,
        recv_sem=recv_sem,
        device_id=device,
        device_id_type=MESH,
    )


def attend(
    heads,
    q_hbm, k_hbm, v_hbm, lists_hbm, w_hbm,
    acc, last_att, last_w,
    q, kv, w, att, pair, lists,
    load_sem, kv_send, kv_recv, w_load, w_send, w_recv, att_send, att_recv,
):
    rows = q.shape[0]
    half = rows // 2
    tile = rows // TILES_DEV
    seq, core = lax.axis_index("seq"), lax.axis_index("head")
    frames = lax.axis_size("seq")
    after, before = lax.rem(seq + 1, frames), lax.rem(seq + frames - 1, frames)
    to_after, to_before, to_sibling = {"seq": after}, {"seq": before}, {"head": 1 - core}

    loads = [
        pltpu.make_async_copy(k_hbm, kv.at[K, OWN], load_sem.at[0]),
        pltpu.make_async_copy(v_hbm, kv.at[V, OWN], load_sem.at[1]),
        pltpu.make_async_copy(q_hbm, q, load_sem.at[2]),
        pltpu.make_async_copy(lists_hbm, lists, load_sem.at[3]),
    ]
    for load in loads:
        load.start()

    barrier = pltpu.get_barrier_semaphore()
    for device in (to_after, to_before, to_sibling):
        pl.semaphore_signal(barrier, inc=1, device_id=device, device_id_type=MESH)
    pl.semaphore_wait(barrier, 3)

    def columns(h):
        return pl.ds(pl.multiple_of(h * HD, HD), HD)

    def kv_copy(h, which, way):
        device, slot = ((to_after, BEFORE), (to_before, AFTER))[way]
        index = (h * 2 + which) * 2 + way
        return remote(
            kv.at[which, OWN, :, columns(h)],
            kv.at[which, slot, :, columns(h)],
            kv_send.at[index],
            kv_recv.at[index],
            device,
        )

    def w_rows(h):
        return pl.ds(pl.multiple_of(h * HD, HD), HD)

    def w_mine(h):
        target = last_w.at[pl.ds(0, HD)] if isinstance(h, int) and h == heads - 1 else w.at[h, pl.ds(0, HD)]
        return pltpu.make_async_copy(w_hbm.at[w_rows(h)], target, w_load.at[h])

    def w_theirs(h):
        target = last_w.at[pl.ds(HD, HD)] if isinstance(h, int) and h == heads - 1 else w.at[h, pl.ds(HD, HD)]
        return remote(w_hbm.at[w_rows(h)], target, w_send.at[h], w_recv.at[h], to_sibling)

    def att_copy(h):
        target = last_att.at[:, pl.ds(HD, HD)] if isinstance(h, int) and h == heads - 1 else pair.at[h, :, pl.ds(HD, HD)]
        return remote(
            att.at[h, pl.ds(pl.multiple_of((1 - core) * half, half), half)],
            target,
            att_send.at[h],
            att_recv.at[h],
            to_sibling,
        )

    loads[0].wait()
    loads[1].wait()
    for h in range(heads):
        for which in (K, V):
            for way in (0, 1):
                kv_copy(h, which, way).start()
    for h in range(heads):
        w_mine(h).start()
        w_theirs(h).start()
    loads[2].wait()
    loads[3].wait()

    picks = []
    for t in range(TILES_DEV):
        lowest = lists[seq * TILES_DEV + t, 0]
        for j in range(1, lists.shape[1]):
            lowest = jnp.minimum(lowest, lists[seq * TILES_DEV + t, j])
        pick = jnp.where(lowest < seq * TILES_DEV, 1, 0)
        picks.append(jnp.full((tile, rows), pick, jnp.int32))
    from_before = jnp.concatenate(picks, axis=0) > 0

    def project(h):
        w_mine(h).wait()
        w_theirs(h).wait()
        att_copy(h).wait()
        term = jnp.dot(pair[h], w[h], preferred_element_type=jnp.float32)
        if isinstance(h, int) and h == 0:
            acc[...] = term
        else:
            acc[...] += term

    def head(h):
        for way in (0, 1):
            kv_copy(h, K, way).wait()
        keys = kv[K, :, :, columns(h)].reshape(3 * rows, HD)
        scores = lax.dot_general(
            q[:, columns(h)], keys, (((1,), (1,)), ((), ())), preferred_element_type=jnp.float32
        ) * (HD**-0.5)
        own = scores[:, :rows]
        other = jnp.where(from_before, scores[:, rows : 2 * rows], scores[:, 2 * rows :])
        peak = jnp.maximum(jnp.max(own, axis=1, keepdims=True), jnp.max(other, axis=1, keepdims=True))
        own, other = jnp.exp(own - peak), jnp.exp(other - peak)
        denominator = jnp.sum(own, axis=1, keepdims=True) + jnp.sum(other, axis=1, keepdims=True)
        weights = jnp.concatenate(
            [own, jnp.where(from_before, other, 0.0), jnp.where(from_before, 0.0, other)], axis=1
        ).astype(jnp.bfloat16)
        if isinstance(h, int):
            if h > 0:
                project(h - 1)
        else:
            project(h - 1)
        for way in (0, 1):
            kv_copy(h, V, way).wait()
        values = kv[V, :, :, columns(h)].reshape(3 * rows, HD)
        summed = jnp.dot(weights, values, preferred_element_type=jnp.float32)
        att[h] = (summed / denominator).astype(jnp.bfloat16)
        att_copy(h).start()
        mine = att[h, pl.ds(pl.multiple_of(core * half, half), half)]
        if isinstance(h, int) and h == heads - 1:
            last_att[:, pl.ds(0, HD)] = mine
        else:
            pair[h, :, pl.ds(0, HD)] = mine

    for h in range(heads):
        head(h)
    w_mine(heads - 1).wait()
    w_theirs(heads - 1).wait()
    att_copy(heads - 1).wait()


def finish(acc, att, w, out):
    out[...] = (acc[...] + jnp.dot(att[...], w[...], preferred_element_type=jnp.float32)).astype(out.dtype)


def on_device(queries, keys, values, tile_lists, out_weight):
    rows, columns = queries.shape
    heads, half, width = columns // HD, rows // 2, out_weight.shape[1]
    bf16 = jnp.bfloat16
    anywhere = pl.BlockSpec(memory_space=pl.ANY)
    in_vmem = pl.BlockSpec(memory_space=pltpu.VMEM)
    dma = pltpu.SemaphoreType.DMA
    acc, att, w = pl.pallas_call(
        functools.partial(attend, heads),
        out_shape=(
            pltpu.VMEM((half, width), jnp.float32),
            pltpu.VMEM((half, 2 * HD), bf16),
            pltpu.VMEM((2 * HD, width), bf16),
        ),
        in_specs=[anywhere] * 5,
        out_specs=(in_vmem, in_vmem, in_vmem),
        scratch_shapes=[
            pltpu.VMEM((rows, columns), bf16),
            pltpu.VMEM((2, 3, rows, columns), bf16),
            pltpu.VMEM((heads, 2 * HD, width), bf16),
            pltpu.VMEM((heads, rows, HD), bf16),
            pltpu.VMEM((heads, half, 2 * HD), bf16),
            pltpu.SMEM(tile_lists.shape, jnp.int32),
            dma((4,)),
            dma((heads * 4,)),
            dma((heads * 4,)),
            dma((heads,)),
            dma((heads,)),
            dma((heads,)),
            dma((heads,)),
            dma((heads,)),
        ],
        compiler_params=pltpu.CompilerParams(
            collective_id=0, has_side_effects=True, vmem_limit_bytes=48 << 20
        ),
        name="attend",
    )(queries, keys, values, tile_lists, out_weight)
    blocks = 4
    return pl.pallas_call(
        finish,
        out_shape=jax.ShapeDtypeStruct((half, width), bf16),
        grid=(blocks,),
        in_specs=[
            pl.BlockSpec((half, width // blocks), lambda i: (0, i)),
            pl.BlockSpec((half, 2 * HD), lambda i: (0, 0)),
            pl.BlockSpec((2 * HD, width // blocks), lambda i: (0, i)),
        ],
        out_specs=pl.BlockSpec((half, width // blocks), lambda i: (0, i)),
        name="finish",
    )(acc, att, w)


def solution(mesh):
    placed = (
        P(("dp", "seq"), "head"),
        P(("dp", "seq"), "head"),
        P(("dp", "seq"), "head"),
        P(),
        P("head", None),
    )
    return jax.shard_map(
        on_device,
        mesh=mesh,
        in_specs=placed,
        out_specs=P(("dp", "seq", "head"), None),
        check_vma=False,
    )
```

time: 72.7 us -> 41.6 us (0.57)
  waiting for transfers between devices: 35.6 us -> 0 us
  Pallas kernels: 0 us -> 34.6 us
  between operations: 13.6 us -> 0.03 us
  matrix products: 9.52 us -> 0 us
  starting transfers between devices: 6.86 us -> 0 us
  other arithmetic: 2.21 us -> 0 us
  local copies, waits for them, and re-layouts: 4.65 us -> 6.7 us
    pallas_call x0 -> x2, Pallas kernels: none -> 34.6 us  [the longest x1 30.5 us: on_device(): pl.pallas_call(functools.partial(attend, heads), out_shape=(pltpu.VMEM((h...]
    reduce_scatter x1 -> x0, waiting for transfers between devices: 25.1 us -> none  [on_device(): lax.psum_scatter(jnp.dot(attended, out_weight, preferred_element_type=jnp...]
    ppermute x2 -> x0, waiting for transfers between devices: 10.4 us -> none  [from_behind(): lax.ppermute(value, axis, [(source, source + steps) for source in range(l...]
    dot_general x7 -> x0, matrix products: 9.52 us -> none  [the longest x3 3.7 us: block_partial(): jnp.einsum('qhk,khd->qhd', weights.astype(jnp.bfloat16), stacked[1], pref...]
    ppermute x2 -> x0, starting transfers between devices: 6.85 us -> none  [from_behind(): lax.ppermute(value, axis, [(source, source + steps) for source in range(l...]
    unnamed x11 -> x13, local copies, waits for them, and re-layouts: 2.54 us -> 6.7 us
    broadcast_in_dim x6 -> x0, local copies, waits for them, and re-layouts: 1.17 us -> none  [the longest x3 0.74 us: block_partial(): jnp.where(allowed_three, jnp.exp(scores - maximum[..., None]), 0.0)]
    another operation x1 -> x0, other arithmetic: 0.95 us -> none  [on_device(): stacked = jnp.stack([keys, values]).reshape(2, token_count, groups, HD)]
  transfers between devices with their start and end apart: 3 -> 0, of which waited for: 2 -> 0; matrix products, arithmetic and copies ran while one was open for 6% -> 0% of each run, Pallas kernels for 0% -> 0%
where the time goes in v1:
time: 41.6 us; the launch traced here: 41.3 us
  Pallas kernels  34.6 us (83%)
  local copies, waits for them, and re-layouts  6.7 us (16%)
    pallas_call x1, Pallas kernels, on_device(): pl.pallas_call(functools.partial(attend, heads), out_shape=(pltpu.VMEM((h...  30.5 us
    unnamed x13, local copies, waits for them, and re-layouts  6.7 us
    pallas_call x1, Pallas kernels, on_device(): pl.pallas_call(finish, out_shape=jax.ShapeDtypeStruct((half, width), bf16...  4.08 us

profile of v1, /device:TPU:1, one launch (start us, length us, event | category | flops | bytes accessed | tf_op | source)
XLA Modules:
  0.0 41.3 jit_solution(18128843772364546744)
XLA Ops:
  0.0 0.8 %copy.6.lists_hbm = s32[128,8]{1,0:T(8,128)S(1)} copy(s32[128,8]{0,1:T(8,128)} %param.8) | data formatting | bytes 8192 | tf_op args[3]
  0.8 0.0 copy-start.2
  0.8 1.0 %copy-done.2 = bf16[256,768]{1,0:T(8,128)(2,1)S(1)} copy-done((bf16[256,768]{1,0:T(8,128)(2,1)S(1)}, bf16[256,768]{1,0:T(8,128)(2,1)}, u32[]{:S(2)}) %copy-start.2) | copy-done | bytes 393240
  1.8 0.0 copy-start.3
  1.8 1.0 %copy-done.3 = bf16[256,768]{1,0:T(8,128)(2,1)S(1)} copy-done((bf16[256,768]{1,0:T(8,128)(2,1)S(1)}, bf16[256,768]{1,0:T(8,128)(2,1)}, u32[]{:S(2)}) %copy-start.3) | copy-done | bytes 393240
  2.8 0.0 copy-start.4
  2.8 1.0 %copy-done.4 = bf16[256,768]{1,0:T(8,128)(2,1)S(1)} copy-done((bf16[256,768]{1,0:T(8,128)(2,1)S(1)}, bf16[256,768]{1,0:T(8,128)(2,1)}, u32[]{:S(2)}) %copy-start.4) | copy-done | bytes 393240
  3.8 30.5 %attend.1 = (f32[128,3072]{1,0:T(8,128)S(1)}, bf16[128,256]{1,0:T(8,128)(2,1)S(1)}, bf16[256,3072]{1,0:T(8,128)(2,1)S(1)}) custom-call(bf16[256,768]{1,0:T(8,128)(2,1)S(1)} %copy-done.2, bf16[256,768]{1,0:T(8,128)(2,1)S(1)} %copy-done.3, bf16[256,768]{1,0:T(8,128)(2,1)S(1)} %copy-done.4, s32[128,8]{1,0:T(8,128)S(1)} %copy.6.lists_hbm, bf16[768,3072]{1,0:T(8,128)(2,1)} %w_hbm.1), custom_call_target="tpu_custom_call" | custom-call | tf_op jit(solution)/shard_map/attend/pallas_call | solution.py:173
  34.3 0.0 copy-start
  34.3 1.1 %copy-done = f32[128,3072]{1,0:T(8,128)} copy-done((f32[128,3072]{1,0:T(8,128)}, f32[128,3072]{1,0:T(8,128)S(1)}, u32[]{:S(2)}) %copy-start) | copy-done | bytes 1572888
  35.4 0.0 copy-start.1
  35.4 1.2 %copy-done.1 = bf16[256,3072]{1,0:T(8,128)(2,1)} copy-done((bf16[256,3072]{1,0:T(8,128)(2,1)}, bf16[256,3072]{1,0:T(8,128)(2,1)S(1)}, u32[]{:S(2)}) %copy-start.1) | copy-done | bytes 1572888
  36.6 0.0 copy-start.5
  36.6 0.6 %copy-done.5 = bf16[128,256]{1,0:T(8,128)(2,1)} copy-done((bf16[128,256]{1,0:T(8,128)(2,1)}, bf16[128,256]{1,0:T(8,128)(2,1)S(1)}, u32[]{:S(2)}) %copy-start.5) | copy-done | bytes 65560
  37.2 4.1 %finish.1 = bf16[128,3072]{1,0:T(8,128)(2,1)} custom-call(f32[128,3072]{1,0:T(8,128)} %copy-done, bf16[128,256]{1,0:T(8,128)(2,1)} %copy-done.5, bf16[256,3072]{1,0:T(8,128)(2,1)} %copy-done.1), custom_call_target="tpu_custom_call" | custom-call | tf_op jit(solution)/shard_map/finish/pallas_call | solution.py:204
Async XLA Ops:
  0.8 1.0 %copy-start.2 = (bf16[256,768]{1,0:T(8,128)(2,1)S(1)}, bf16[256,768]{1,0:T(8,128)(2,1)}, u32[]{:S(2)}) copy-start(bf16[256,768]{1,0:T(8,128)(2,1)} %q_hbm.1) | copy-start | bytes 1179652
  1.8 1.0 %copy-start.3 = (bf16[256,768]{1,0:T(8,128)(2,1)S(1)}, bf16[256,768]{1,0:T(8,128)(2,1)}, u32[]{:S(2)}) copy-start(bf16[256,768]{1,0:T(8,128)(2,1)} %k_hbm.1) | copy-start | bytes 1179652
  2.8 1.0 %copy-start.4 = (bf16[256,768]{1,0:T(8,128)(2,1)S(1)}, bf16[256,768]{1,0:T(8,128)(2,1)}, u32[]{:S(2)}) copy-start(bf16[256,768]{1,0:T(8,128)(2,1)} %v_hbm.1) | copy-start | bytes 1179652
  34.3 1.2 %copy-start = (f32[128,3072]{1,0:T(8,128)}, f32[128,3072]{1,0:T(8,128)S(1)}, u32[]{:S(2)}) copy-start(f32[128,3072]{1,0:T(8,128)S(1)} %get-tuple-element.8.acc) | copy-start | bytes 4718596
  35.4 1.2 %copy-start.1 = (bf16[256,3072]{1,0:T(8,128)(2,1)}, bf16[256,3072]{1,0:T(8,128)(2,1)S(1)}, u32[]{:S(2)}) copy-start(bf16[256,3072]{1,0:T(8,128)(2,1)S(1)} %get-tuple-element.10.w) | copy-start | bytes 4718596
  36.6 0.6 %copy-start.5 = (bf16[128,256]{1,0:T(8,128)(2,1)}, bf16[128,256]{1,0:T(8,128)(2,1)S(1)}, u32[]{:S(2)}) copy-start(bf16[128,256]{1,0:T(8,128)(2,1)S(1)} %get-tuple-element.9.att) | copy-start | bytes 196612

commit v2 on v1

v2 whole, which is shorter than its diff:
```python
import functools

import jax
import jax.numpy as jnp
from jax import lax
from jax.experimental import pallas as pl
from jax.experimental.pallas import tpu as pltpu
from jax.sharding import PartitionSpec as P

HD = 128
TILES_DEV = 4
MESH = pl.DeviceIdType.MESH
OWN, BEFORE, AFTER = 0, 1, 2
K, V = 0, 1


def remote(src, dst, send_sem, recv_sem, device):
    return pltpu.make_async_remote_copy(
        src_ref=src,
        dst_ref=dst,
        send_sem=send_sem,
        recv_sem=recv_sem,
        device_id=device,
        device_id_type=MESH,
    )


def attend(
    heads,
    q_hbm, k_hbm, v_hbm, lists_hbm, w_hbm,
    acc, last_att, last_w,
    q, kv, w, whole, att, pair, lists,
    load_sem, kv_send, kv_recv, w_load, w_send, w_recv, att_send, att_recv,
):
    rows = q.shape[0]
    half = rows // 2
    tile = rows // TILES_DEV
    last = heads - 1
    seq, core = lax.axis_index("seq"), lax.axis_index("head")
    frames = lax.axis_size("seq")
    has_before, has_after = seq > 0, seq < frames - 1
    to_before = {"seq": jnp.maximum(seq - 1, 0)}
    to_after = {"seq": jnp.minimum(seq + 1, frames - 1)}
    to_sibling = {"head": 1 - core}
    ways = ((to_after, BEFORE, has_after, has_before), (to_before, AFTER, has_before, has_after))

    barrier = pltpu.get_barrier_semaphore()
    for device, _, sends, _ in ways:

        @pl.when(sends)
        def _(device=device):
            pl.semaphore_signal(barrier, inc=1, device_id=device, device_id_type=MESH)

    pl.semaphore_signal(barrier, inc=1, device_id=to_sibling, device_id_type=MESH)

    def columns(h):
        return pl.ds(h * HD, HD)

    loads = []
    for source, which in ((k_hbm, K), (v_hbm, V)):
        for start, width in ((0, 1), (1, heads - 1)):
            part = pl.ds(start * HD, width * HD)
            loads.append(
                (start, which, pltpu.make_async_copy(source.at[:, part], kv.at[which, OWN, :, part], load_sem.at[len(loads)]))
            )
    loads.sort(key=lambda x: x[:2])
    q_load = pltpu.make_async_copy(q_hbm, q, load_sem.at[2 * heads])
    lists_load = pltpu.make_async_copy(lists_hbm, lists, load_sem.at[2 * heads + 1])
    for _, _, load in loads:
        load.start()
    q_load.start()
    lists_load.start()

    pl.semaphore_wait(barrier, 1 + has_before.astype(jnp.int32) + has_after.astype(jnp.int32))

    def kv_copy(h, which, way):
        device, slot, _, _ = ways[way]
        index = (h * 2 + which) * 2 + way
        source = kv.at[which, OWN, :, columns(h)]
        return remote(
            source,
            kv.at[which, slot, :, columns(h)],
            kv_send.at[index],
            kv_recv.at[index],
            device,
        )

    def kv_arrive(h, which):
        for way in (0, 1):

            @pl.when(ways[way][3])
            def _():
                kv_copy(h, which, way).wait_recv()

    def kv_sent(h, which):
        for way in (0, 1):

            @pl.when(ways[way][2])
            def _():
                kv_copy(h, which, way).wait_send()

    def w_mine(h):
        target = last_w.at[pl.ds(0, HD)] if h == last else w.at[h, pl.ds(0, HD)]
        return pltpu.make_async_copy(w_hbm.at[pl.ds(h * HD, HD)], target, w_load.at[h])

    def w_theirs(h):
        target = last_w.at[pl.ds(HD, HD)] if h == last else w.at[h, pl.ds(HD, HD)]
        return remote(w_hbm.at[pl.ds(h * HD, HD)], target, w_send.at[h], w_recv.at[h], to_sibling)

    def att_copy(h):
        target = last_att.at[:, pl.ds(HD, HD)] if h == last else pair.at[h, :, pl.ds(HD, HD)]
        return remote(att.at[h], target, att_send.at[h], att_recv.at[h], to_sibling)

    order = [(h, which) for h in range(heads) for which in (K, V)]
    for h, which in order:
        for start, kind, load in loads:
            if (start, kind) == (h, which):
                load.wait()
        for way in (0, 1):

            @pl.when(ways[way][2])
            def _():
                kv_copy(h, which, way).start()
    for h in range(heads):
        w_mine(h).start()
        w_theirs(h).start()

    for slot, there in ((BEFORE, has_before), (AFTER, has_after)):

        @pl.when(jnp.logical_not(there))
        def _():
            kv[:, slot] = jnp.zeros((2, *kv.shape[2:]), kv.dtype)

    q_load.wait()
    lists_load.wait()

    picks = []
    for t in range(TILES_DEV):
        lowest = lists[0, seq * TILES_DEV + t]
        for j in range(1, lists.shape[0]):
            lowest = jnp.minimum(lowest, lists[j, seq * TILES_DEV + t])
        pick = jnp.where(lowest < seq * TILES_DEV, 1, 0)
        picks.append(jnp.full((tile, rows), pick, jnp.int32))
    from_before = jnp.concatenate(picks, axis=0) > 0

    def project(h):
        w_mine(h).wait()
        w_theirs(h).wait()
        att_copy(h).wait()
        term = jnp.dot(pair[h], w[h], preferred_element_type=jnp.float32)
        if h == 0:
            acc[...] = term
        else:
            acc[...] += term

    theirs, mine = (pl.ds(pl.multiple_of(part * half, half), half) for part in (1 - core, core))
    for h in range(heads):
        kv_arrive(h, K)
        keys = kv[K, :, :, columns(h)].reshape(3 * rows, HD)
        scores = lax.dot_general(
            q[:, columns(h)], keys, (((1,), (1,)), ((), ())), preferred_element_type=jnp.float32
        ) * (HD**-0.5)
        own = scores[:, :rows]
        other = jnp.where(from_before, scores[:, rows : 2 * rows], scores[:, 2 * rows :])
        peak = jnp.maximum(jnp.max(own, axis=1, keepdims=True), jnp.max(other, axis=1, keepdims=True))
        own, other = jnp.exp(own - peak), jnp.exp(other - peak)
        denominator = jnp.sum(own, axis=1, keepdims=True) + jnp.sum(other, axis=1, keepdims=True)
        weights = jnp.concatenate(
            [own, jnp.where(from_before, other, 0.0), jnp.where(from_before, 0.0, other)], axis=1
        ).astype(jnp.bfloat16)
        if h > 0:
            project(h - 1)
        kv_sent(h, K)
        kv_arrive(h, V)
        values = kv[V, :, :, columns(h)].reshape(3 * rows, HD)
        summed = jnp.dot(weights, values, preferred_element_type=jnp.float32)
        whole[...] = (summed / denominator).astype(jnp.bfloat16)
        att[h] = whole[theirs]
        att_copy(h).start()
        if h == last:
            last_att[:, pl.ds(0, HD)] = whole[mine]
        else:
            pair[h, :, pl.ds(0, HD)] = whole[mine]
        kv_sent(h, V)
    w_mine(last).wait()
    w_theirs(last).wait()
    att_copy(last).wait()


def finish(blocks, acc, att, w, out, rounded, sem):
    width = out.shape[1] // blocks
    copies = []
    for b in range(blocks):
        part = pl.ds(b * width, width)
        total = acc[:, part] + jnp.dot(att[...], w[:, part], preferred_element_type=jnp.float32)
        rounded[:, part] = total.astype(out.dtype)
        copies.append(pltpu.make_async_copy(rounded.at[:, part], out.at[:, part], sem.at[b]))
        copies[-1].start()
    for copy in copies:
        copy.wait()


def on_device(queries, keys, values, tile_lists, out_weight):
    rows, columns = queries.shape
    heads, half, width = columns // HD, rows // 2, out_weight.shape[1]
    bf16 = jnp.bfloat16
    anywhere = pl.BlockSpec(memory_space=pl.ANY)
    in_vmem = pl.BlockSpec(memory_space=pltpu.VMEM)
    dma = pltpu.SemaphoreType.DMA
    kept = [
        pltpu.with_memory_space_constraint(x, pltpu.HBM)
        for x in (queries, keys, values, tile_lists.T, out_weight)
    ]
    acc, att, w = pl.pallas_call(
        functools.partial(attend, heads),
        out_shape=(
            pltpu.VMEM((half, width), jnp.float32),
            pltpu.VMEM((half, 2 * HD), bf16),
            pltpu.VMEM((2 * HD, width), bf16),
        ),
        in_specs=[pl.BlockSpec(memory_space=pltpu.HBM)] * 5,
        out_specs=(in_vmem, in_vmem, in_vmem),
        scratch_shapes=[
            pltpu.VMEM((rows, columns), bf16),
            pltpu.VMEM((2, 3, rows, columns), bf16),
            pltpu.VMEM((heads, 2 * HD, width), bf16),
            pltpu.VMEM((rows, HD), bf16),
            pltpu.VMEM((heads, half, HD), bf16),
            pltpu.VMEM((heads, half, 2 * HD), bf16),
            pltpu.SMEM(kept[3].shape, jnp.int32),
            dma((2 * heads + 2,)),
            dma((heads * 4,)),
            dma((heads * 4,)),
            dma((heads,)),
            dma((heads,)),
            dma((heads,)),
            dma((heads,)),
            dma((heads,)),
        ],
        compiler_params=pltpu.CompilerParams(
            collective_id=0, has_side_effects=True, vmem_limit_bytes=48 << 20
        ),
        name="attend",
    )(*kept)
    blocks = 4
    return pl.pallas_call(
        functools.partial(finish, blocks),
        out_shape=jax.ShapeDtypeStruct((half, width), bf16),
        in_specs=[in_vmem] * 3,
        out_specs=anywhere,
        scratch_shapes=[pltpu.VMEM((half, width), bf16), dma((blocks,))],
        name="finish",
    )(*(pltpu.with_memory_space_constraint(x, pltpu.VMEM) for x in (acc, att, w)))


def solution(mesh):
    placed = (
        P(("dp", "seq"), "head"),
        P(("dp", "seq"), "head"),
        P(("dp", "seq"), "head"),
        P(),
        P("head", None),
    )
    return jax.shard_map(
        on_device,
        mesh=mesh,
        in_specs=placed,
        out_specs=P(("dp", "seq", "head"), None),
        check_vma=False,
    )
```

time: 41.6 us -> 26.5 us (0.64)
  the two profiles are of different devices: /device:TPU:1 before, /device:TPU:129 now
where the time goes in v2:
time: 26.5 us
  Pallas kernels  26.4 us (100%)
    pallas_call x1, Pallas kernels, on_device(): pl.pallas_call(functools.partial(attend, heads), out_shape=(pltpu.VMEM((h...  25.3 us
    pallas_call x1, Pallas kernels, on_device(): pl.pallas_call(functools.partial(finish, blocks), out_shape=jax.ShapeDtyp...  1.16 us

profile of v2, /device:TPU:129, one launch (start us, length us, event | category | flops | bytes accessed | tf_op | source)
XLA Modules:
  0.0 26.5 jit_solution(17831737599245470254)
XLA Ops:
  0.0 25.3 %attend.1 = (f32[128,3072]{1,0:T(8,128)S(1)}, bf16[128,256]{1,0:T(8,128)(2,1)S(1)}, bf16[256,3072]{1,0:T(8,128)(2,1)S(1)}) custom-call(bf16[256,768]{1,0:T(8,128)(2,1)} %q_hbm.1, bf16[256,768]{1,0:T(8,128)(2,1)} %k_hbm.1, bf16[256,768]{1,0:T(8,128)(2,1)} %v_hbm.1, s32[8,128]{1,0:T(8,128)} %bitcast.1, bf16[768,3072]{1,0:T(8,128)(2,1)} %w_hbm.1), custom_call_target="tpu_custom_call" | custom-call | tf_op jit(solution)/shard_map/attend/pallas_call | solution.py:214
  25.3 1.2 %finish.1 = bf16[128,3072]{1,0:T(8,128)(2,1)} custom-call(f32[128,3072]{1,0:T(8,128)S(1)} %get-tuple-element.8.acc, bf16[128,256]{1,0:T(8,128)(2,1)S(1)} %get-tuple-element.9.att, bf16[256,3072]{1,0:T(8,128)(2,1)S(1)} %get-tuple-element.10.w), custom_call_target="tpu_custom_call" | custom-call | tf_op jit(solution)/shard_map/finish/pallas_call | solution.py:246

commit v3 on v2

v3 whole, which is shorter than its diff:
```python
import functools

import jax
import jax.numpy as jnp
from jax import lax
from jax.experimental import pallas as pl
from jax.experimental.pallas import tpu as pltpu
from jax.sharding import PartitionSpec as P

HD = 128
TILES_DEV = 4
MESH = pl.DeviceIdType.MESH
OWN, BEFORE, AFTER = 0, 1, 2
K, V = 0, 1
LATE = 3


def remote(src, dst, send_sem, recv_sem, device):
    return pltpu.make_async_remote_copy(
        src_ref=src,
        dst_ref=dst,
        send_sem=send_sem,
        recv_sem=recv_sem,
        device_id=device,
        device_id_type=MESH,
    )


def attend(
    heads,
    q_hbm, k_hbm, v_hbm, lists_hbm, w_hbm,
    acc, last_att, last_w,
    q, late_q, kv, w, whole, att, pair, part_out, part_mid, part_in, own_out, own_in,
    log_out, log_mid, log_in, lists,
    load_sem, kv_send, kv_recv, q_send, q_recv, att_send, att_recv, w_load, w_send, w_recv,
    swap_send, swap_recv, own_send, own_recv, part_send, part_recv, log_send, log_recv, pass_send, pass_recv,
):
    rows = q.shape[0]
    half = rows // 2
    tile = rows // TILES_DEV
    early = heads - LATE
    last = heads - 1
    scale = HD**-0.5
    seq, core = lax.axis_index("seq"), lax.axis_index("head")
    frames = lax.axis_size("seq")
    has_before, has_after = seq > 0, seq < frames - 1
    sibling = {"head": 1 - core}
    ways = (
        ({"seq": jnp.minimum(seq + 1, frames - 1)}, BEFORE, has_after, has_before),
        ({"seq": jnp.maximum(seq - 1, 0)}, AFTER, has_before, has_after),
    )

    barrier = pltpu.get_barrier_semaphore()
    for device, _, there, _ in ways:

        @pl.when(there)
        def _(device=device):
            pl.semaphore_signal(barrier, inc=1, device_id=device, device_id_type=MESH)

    pl.semaphore_signal(barrier, inc=1, device_id=sibling, device_id_type=MESH)

    loads = [
        pltpu.make_async_copy(source, target, load_sem.at[i])
        for i, (source, target) in enumerate(
            ((q_hbm, q), (k_hbm, kv.at[K, OWN]), (v_hbm, kv.at[V, OWN]), (lists_hbm, lists))
        )
    ]
    for load in loads:
        load.start()

    pl.semaphore_wait(barrier, 1 + has_before.astype(jnp.int32) + has_after.astype(jnp.int32))

    def columns(h):
        return pl.ds(h * HD, HD)

    def kv_copy(h, which, way):
        device, slot = ways[way][:2]
        index = (h * 2 + which) * 2 + way
        return remote(
            kv.at[which, OWN, :, columns(h)],
            kv.at[which, slot, :, columns(h)],
            kv_send.at[index],
            kv_recv.at[index],
            device,
        )

    def q_copy(i, way):
        device, slot = ways[way][:2]
        index = i * 2 + way
        return remote(
            q.at[:, columns(early + i)], late_q.at[i, slot - 1], q_send.at[index], q_recv.at[index], device
        )

    def part_copy(i, way):
        device, slot = ways[way][:2]
        index = i * 2 + way
        return remote(
            part_mid.at[i, way], part_in.at[i, slot - 1], part_send.at[index], part_recv.at[index], device
        )

    def log_copy(way):
        device, slot = ways[way][:2]
        return remote(log_mid.at[1 + way], log_in.at[slot - 1], log_send.at[way], log_recv.at[way], device)

    def start(copy_of, *which):
        for way in (0, 1):

            @pl.when(ways[way][2])
            def _():
                copy_of(*which, way).start()

    def sent(copy_of, *which):
        for way in (0, 1):

            @pl.when(ways[way][2])
            def _():
                copy_of(*which, way).wait_send()

    def arrive(copy_of, *which):
        for way in (0, 1):

            @pl.when(ways[way][3])
            def _():
                copy_of(*which, way).wait_recv()

    def w_target(h, at):
        return last_w.at[pl.ds(at * HD, HD)] if h == last else w.at[h, pl.ds(at * HD, HD)]

    def w_mine(h):
        return pltpu.make_async_copy(w_hbm.at[pl.ds(h * HD, HD)], w_target(h, 0), w_load.at[h])

    def w_swap(h):
        return remote(w_hbm.at[pl.ds(h * HD, HD)], w_target(h, 1), w_send.at[h], w_recv.at[h], sibling)

    def att_swap(h):
        return remote(att.at[h], pair.at[h, :, pl.ds(HD, HD)], att_send.at[h], att_recv.at[h], sibling)

    def part_swap(i):
        return remote(
            part_out.at[i, 1 - core], part_mid.at[i, :, pl.ds(HD, HD)], swap_send.at[i], swap_recv.at[i], sibling
        )

    def own_swap(i):
        return remote(own_out.at[i, 1 - core], own_in.at[i, pl.ds(HD, HD)], own_send.at[i], own_recv.at[i], sibling)

    def log_swap():
        return remote(log_out.at[1 - core], log_mid.at[:, 1], pass_send, pass_recv, sibling)

    loads[0].wait()
    for i in range(LATE):
        start(q_copy, i)
    loads[1].wait()
    loads[2].wait()
    for h in range(early):
        start(kv_copy, h, K)
        start(kv_copy, h, V)
    for h in range(heads):
        w_mine(h).start()
        w_swap(h).start()
    loads[3].wait()

    for slot, there in ((BEFORE, has_before), (AFTER, has_after)):

        @pl.when(jnp.logical_not(there))
        def _():
            kv[:, slot] = jnp.zeros((2, *kv.shape[2:]), kv.dtype)

    picks = []
    for t in range(TILES_DEV):
        lowest = lists[0, seq * TILES_DEV + t]
        for j in range(1, lists.shape[0]):
            lowest = jnp.minimum(lowest, lists[j, seq * TILES_DEV + t])
        picks.append(jnp.where(lowest < seq * TILES_DEV, 1, 0))
    from_before = (
        jnp.concatenate([jnp.full((tile, rows), pick, jnp.int32) for pick in picks], axis=0) > 0
    )
    place = lax.broadcasted_iota(jnp.int32, (1, half), 1)
    picked = jnp.zeros((1, half), jnp.int32)
    half_tiles = TILES_DEV // 2
    for t in range(half_tiles):
        pick = jnp.where(core == 0, picks[t], picks[half_tiles + t])
        inside = jnp.logical_and(place >= t * tile, place < (t + 1) * tile)
        picked = jnp.where(inside, pick, picked)
    mine_before = picked > 0

    def serve(i):
        h = early + i
        arrive(q_copy, i)
        queries = jnp.concatenate([q[:, columns(h)], late_q[i, 0], late_q[i, 1]], axis=0)
        scores = lax.dot_general(
            kv[K, OWN, :, columns(h)], queries, (((1,), (1,)), ((), ())), preferred_element_type=jnp.float32
        ) * scale
        peak = jnp.max(scores, axis=0, keepdims=True)
        weights = jnp.exp(scores - peak)
        denominator = jnp.sum(weights, axis=0, keepdims=True)
        logs = peak + jnp.log(denominator)
        part = lax.dot_general(
            kv[V, OWN, :, columns(h)],
            weights.astype(jnp.bfloat16),
            (((0,), (0,)), ((), ())),
            preferred_element_type=jnp.float32,
        ) * (1.0 / denominator)
        for slot, frame in ((OWN, 0), (1, AFTER), (2, BEFORE)):
            for whose in (0, 1):
                first = frame * rows + whose * half
                if slot == OWN:
                    own_out[i, whose] = part[:, first : first + half]
                else:
                    part_out[i, whose, slot - 1] = part[:, first : first + half].astype(jnp.bfloat16)
                log_out[whose, slot, i] = logs[:, first : first + half]
        part_swap(i).start()
        own_swap(i).start()
        for way in (0, 1):
            part_mid[i, way, pl.ds(0, HD)] = part_out[i, core, way]

    def answer():
        log_swap().wait_recv()
        start(log_copy)
        for i in range(LATE):
            part_swap(i).wait_recv()
            start(part_copy, i)

    def project(h, both):
        w_mine(h).wait()
        w_swap(h).wait()
        term = jnp.dot(both, w[h], preferred_element_type=jnp.float32)
        if h == 0:
            acc[...] = term
        else:
            acc[...] += term

    theirs, mine = (pl.ds(pl.multiple_of(part * half, half), half) for part in (1 - core, core))

    def early_head(h):
        arrive(kv_copy, h, K)
        keys = kv[K, :, :, columns(h)].reshape(3 * rows, HD)
        scores = lax.dot_general(
            q[:, columns(h)], keys, (((1,), (1,)), ((), ())), preferred_element_type=jnp.float32
        ) * scale
        own = scores[:, :rows]
        other = jnp.where(from_before, scores[:, rows : 2 * rows], scores[:, 2 * rows :])
        peak = jnp.maximum(jnp.max(own, axis=1, keepdims=True), jnp.max(other, axis=1, keepdims=True))
        own, other = jnp.exp(own - peak), jnp.exp(other - peak)
        denominator = jnp.sum(own, axis=1, keepdims=True) + jnp.sum(other, axis=1, keepdims=True)
        weights = jnp.concatenate(
            [own, jnp.where(from_before, other, 0.0), jnp.where(from_before, 0.0, other)], axis=1
        ).astype(jnp.bfloat16)
        if h > 0:
            att_swap(h - 1).wait()
            project(h - 1, pair[h - 1])
        sent(kv_copy, h, K)
        arrive(kv_copy, h, V)
        values = kv[V, :, :, columns(h)].reshape(3 * rows, HD)
        summed = jnp.dot(weights, values, preferred_element_type=jnp.float32)
        whole[...] = (summed / denominator).astype(jnp.bfloat16)
        att[h] = whole[theirs]
        att_swap(h).start()
        pair[h, :, pl.ds(0, HD)] = whole[mine]
        sent(kv_copy, h, V)

    def shares(i):
        out = []
        for whose in (0, 1):
            other = jnp.where(mine_before, log_in[0, whose, i], log_in[1, whose, i])
            out.append(1.0 / (1.0 + jnp.exp(log_mid[OWN, whose, i] - other)))
        return out

    def merge(i, share):
        arrive(part_copy, i)
        merged = []
        for whose in (0, 1):
            some = pl.ds(whose * HD, HD)
            own = own_out[i, core] if whose == 0 else own_in[i, some]
            other = jnp.where(mine_before, part_in[i, 0, some], part_in[i, 1, some]).astype(jnp.float32)
            merged.append(own + share[whose] * (other - own))
        return jnp.concatenate(merged, axis=0).T.astype(jnp.bfloat16)

    for i in range(LATE):
        serve(i)
    log_swap().start()
    for slot in (OWN, 1, 2):
        log_mid[slot, 0] = log_out[core, slot]
    for h in range(early):
        early_head(h)
        if h == 0:
            answer()
    att_swap(early - 1).wait()
    project(early - 1, pair[early - 1])
    log_swap().wait_send()
    for i in range(LATE):
        own_swap(i).wait()
        part_swap(i).wait_send()
        sent(q_copy, i)
    sent(log_copy)
    arrive(log_copy)
    share = [shares(i) for i in range(LATE)]
    w_mine(last).wait()
    w_swap(last).wait()
    for i in range(LATE):
        both = merge(i, share[i])
        if early + i < last:
            project(early + i, both)
        else:
            last_att[...] = both
        sent(part_copy, i)


def finish(blocks, acc, att, w, out, rounded, sem):
    width = out.shape[1] // blocks
    copies = []
    for b in range(blocks):
        part = pl.ds(b * width, width)
        total = acc[:, part] + jnp.dot(att[...], w[:, part], preferred_element_type=jnp.float32)
        rounded[:, part] = total.astype(out.dtype)
        copies.append(pltpu.make_async_copy(rounded.at[:, part], out.at[:, part], sem.at[b]))
        copies[-1].start()
    for copy in copies:
        copy.wait()


def on_device(queries, keys, values, tile_lists, out_weight):
    rows, columns = queries.shape
    heads, half, width = columns // HD, rows // 2, out_weight.shape[1]
    early = heads - LATE
    bf16, f32 = jnp.bfloat16, jnp.float32
    anywhere = pl.BlockSpec(memory_space=pl.ANY)
    in_vmem = pl.BlockSpec(memory_space=pltpu.VMEM)
    dma = pltpu.SemaphoreType.DMA
    kept = [
        pltpu.with_memory_space_constraint(x, pltpu.HBM)
        for x in (queries, keys, values, tile_lists.T, out_weight)
    ]
    acc, att, w = pl.pallas_call(
        functools.partial(attend, heads),
        out_shape=(
            pltpu.VMEM((half, width), f32),
            pltpu.VMEM((half, 2 * HD), bf16),
            pltpu.VMEM((2 * HD, width), bf16),
        ),
        in_specs=[pl.BlockSpec(memory_space=pltpu.HBM)] * 5,
        out_specs=(in_vmem, in_vmem, in_vmem),
        scratch_shapes=[
            pltpu.VMEM((rows, columns), bf16),
            pltpu.VMEM((LATE, 2, rows, HD), bf16),
            pltpu.VMEM((2, 3, rows, columns), bf16),
            pltpu.VMEM((heads - 1, 2 * HD, width), bf16),
            pltpu.VMEM((rows, HD), bf16),
            pltpu.VMEM((early, half, HD), bf16),
            pltpu.VMEM((early, half, 2 * HD), bf16),
            pltpu.VMEM((LATE, 2, 2, HD, half), bf16),
            pltpu.VMEM((LATE, 2, 2 * HD, half), bf16),
            pltpu.VMEM((LATE, 2, 2 * HD, half), bf16),
            pltpu.VMEM((LATE, 2, HD, half), f32),
            pltpu.VMEM((LATE, 2 * HD, half), f32),
            pltpu.VMEM((2, 3, LATE, 1, half), f32),
            pltpu.VMEM((3, 2, LATE, 1, half), f32),
            pltpu.VMEM((2, 2, LATE, 1, half), f32),
            pltpu.SMEM(kept[3].shape, jnp.int32),
            dma((4,)),
            dma((early * 4,)),
            dma((early * 4,)),
            dma((LATE * 2,)),
            dma((LATE * 2,)),
            dma((early,)),
            dma((early,)),
            dma((heads,)),
            dma((heads,)),
            dma((heads,)),
            dma((LATE,)),
            dma((LATE,)),
            dma((LATE,)),
            dma((LATE,)),
            dma((LATE * 2,)),
            dma((LATE * 2,)),
            dma((2,)),
            dma((2,)),
            dma,
            dma,
        ],
        compiler_params=pltpu.CompilerParams(
            collective_id=0, has_side_effects=True, vmem_limit_bytes=48 << 20
        ),
        name="attend",
    )(*kept)
    blocks = 4
    return pl.pallas_call(
        functools.partial(finish, blocks),
        out_shape=jax.ShapeDtypeStruct((half, width), bf16),
        in_specs=[in_vmem] * 3,
        out_specs=anywhere,
        scratch_shapes=[pltpu.VMEM((half, width), bf16), dma((blocks,))],
        name="finish",
    )(*(pltpu.with_memory_space_constraint(x, pltpu.VMEM) for x in (acc, att, w)))


def solution(mesh):
    placed = (
        P(("dp", "seq"), "head"),
        P(("dp", "seq"), "head"),
        P(("dp", "seq"), "head"),
        P(),
        P("head", None),
    )
    return jax.shard_map(
        on_device,
        mesh=mesh,
        in_specs=placed,
        out_specs=P(("dp", "seq", "head"), None),
        check_vma=False,
    )
```

time: 26.5 us -> 24.9 us (0.940)
  the two profiles are of different devices: /device:TPU:129 before, /device:TPU:124 now
where the time goes in v3:
time: 24.9 us; the launch traced here: 24.8 us
  Pallas kernels  24.8 us (100%)
    pallas_call x1, Pallas kernels, on_device(): pl.pallas_call(functools.partial(attend, heads), out_shape=(pltpu.VMEM((h...  23.6 us
    pallas_call x1, Pallas kernels, on_device(): pl.pallas_call(functools.partial(finish, blocks), out_shape=jax.ShapeDtyp...  1.16 us

profile of v3, /device:TPU:124, one launch (start us, length us, event | category | flops | bytes accessed | tf_op | source)
XLA Modules:
  0.0 24.8 jit_solution(7793262343988440076)
XLA Ops:
  0.0 23.6 %attend.1 = (f32[128,3072]{1,0:T(8,128)S(1)}, bf16[128,256]{1,0:T(8,128)(2,1)S(1)}, bf16[256,3072]{1,0:T(8,128)(2,1)S(1)}) custom-call(bf16[256,768]{1,0:T(8,128)(2,1)} %q_hbm.1, bf16[256,768]{1,0:T(8,128)(2,1)} %k_hbm.1, bf16[256,768]{1,0:T(8,128)(2,1)} %v_hbm.1, s32[8,128]{1,0:T(8,128)} %bitcast.1, bf16[768,3072]{1,0:T(8,128)(2,1)} %w_hbm.1), custom_call_target="tpu_custom_call" | custom-call | tf_op jit(solution)/shard_map/attend/pallas_call | solution.py:333
  23.6 1.2 %finish.1 = bf16[128,3072]{1,0:T(8,128)(2,1)} custom-call(f32[128,3072]{1,0:T(8,128)S(1)} %get-tuple-element.8.acc, bf16[128,256]{1,0:T(8,128)(2,1)S(1)} %get-tuple-element.9.att, bf16[256,3072]{1,0:T(8,128)(2,1)S(1)} %get-tuple-element.10.w), custom_call_target="tpu_custom_call" | custom-call | tf_op jit(solution)/shard_map/finish/pallas_call | solution.py:386

commit v4 on v3

--- a/solution.py
+++ b/solution.py
@@ -13,6 +13,9 @@
 OWN, BEFORE, AFTER = 0, 1, 2
 K, V = 0, 1
 LATE = 3
+RING = 4
+AT_ONCE = 3
+RELAYED = 128
 
 
 def remote(src, dst, send_sem, recv_sem, device):
@@ -31,9 +34,10 @@
     q_hbm, k_hbm, v_hbm, lists_hbm, w_hbm,
     acc, last_att, last_w,
     q, late_q, kv, w, whole, att, pair, part_out, part_mid, part_in, own_out, own_in,
-    log_out, log_mid, log_in, lists,
+    log_out, log_mid, log_in, relay, lists,
     load_sem, kv_send, kv_recv, q_send, q_recv, att_send, att_recv, w_load, w_send, w_recv,
     swap_send, swap_recv, own_send, own_recv, part_send, part_recv, log_send, log_recv, pass_send, pass_recv,
+    piece_send, piece_recv, relay_send, relay_recv,
 ):
     rows = q.shape[0]
     half = rows // 2
@@ -50,6 +54,16 @@
         ({"seq": jnp.maximum(seq - 1, 0)}, AFTER, has_before, has_after),
     )
 
+    place = lax.rem(seq, RING)
+    next_ring, last_ring = seq < frames - RING, seq >= RING
+    joins = ((0, jnp.logical_and(place == 3, next_ring)), (1, jnp.logical_and(place == 0, last_ring)))
+    near = ((0, jnp.logical_and(place == 2, next_ring)), (1, jnp.logical_and(place == 1, last_ring)))
+    far = ((0, jnp.logical_and(place == 1, next_ring)), (1, jnp.logical_and(place == 2, last_ring)))
+    over = (
+        {"seq": jnp.minimum(seq + RING - 1, frames - 1)},
+        {"seq": jnp.maximum(seq - RING + 1, 0)},
+    )
+
     barrier = pltpu.get_barrier_semaphore()
     for device, _, there, _ in ways:
 
@@ -73,16 +87,37 @@
     def columns(h):
         return pl.ds(h * HD, HD)
 
+    size = relay.shape[1]
+    piece_at = (V, pl.ds(0, size), columns(early - 1))
+
     def kv_copy(h, which, way):
         device, slot = ways[way][:2]
         index = (h * 2 + which) * 2 + way
+        some = pl.ds(size, rows - size) if (h, which) == (early - 1, V) else pl.ds(0, rows)
         return remote(
-            kv.at[which, OWN, :, columns(h)],
-            kv.at[which, slot, :, columns(h)],
+            kv.at[which, OWN, some, columns(h)],
+            kv.at[which, slot, some, columns(h)],
             kv_send.at[index],
             kv_recv.at[index],
             device,
         )
+
+    def piece(slot):
+        return kv.at[piece_at[0], slot, piece_at[1], piece_at[2]]
+
+    def piece_copy(way):
+        device, slot = ways[way][:2]
+        return remote(piece(OWN), piece(slot), piece_send.at[way], piece_recv.at[way], device)
+
+    def to_relay(way):
+        return remote(piece(OWN), relay.at[way], piece_send.at[way], relay_recv.at[way], ways[1 - way][0])
+
+    def relay_on(way):
+        return remote(relay.at[way], relay.at[way], relay_send.at[way], relay_recv.at[way], ways[1 - way][0])
+
+    def relay_out(way):
+        slot = ways[way][1]
+        return remote(relay.at[way], piece(slot), relay_send.at[way], piece_recv.at[way], over[way])
 
     def q_copy(i, way):
         device, slot = ways[way][:2]
@@ -146,14 +181,19 @@
     def log_swap():
         return remote(log_out.at[1 - core], log_mid.at[:, 1], pass_send, pass_recv, sibling)
 
-    loads[0].wait()
+    for load in loads[:3]:
+        load.wait()
+    for way, there in joins:
+
+        @pl.when(there)
+        def _():
+            to_relay(way).start()
+
     for i in range(LATE):
         start(q_copy, i)
-    loads[1].wait()
-    loads[2].wait()
-    for h in range(early):
-        start(kv_copy, h, K)
-        start(kv_copy, h, V)
+    queue = [(h, which) for h in range(early) for which in (K, V)]
+    for h, which in queue[:AT_ONCE]:
+        start(kv_copy, h, which)
     for h in range(heads):
         w_mine(h).start()
         w_swap(h).start()
@@ -174,12 +214,12 @@
     from_before = (
         jnp.concatenate([jnp.full((tile, rows), pick, jnp.int32) for pick in picks], axis=0) > 0
     )
-    place = lax.broadcasted_iota(jnp.int32, (1, half), 1)
+    token = lax.broadcasted_iota(jnp.int32, (1, half), 1)
     picked = jnp.zeros((1, half), jnp.int32)
     half_tiles = TILES_DEV // 2
     for t in range(half_tiles):
         pick = jnp.where(core == 0, picks[t], picks[half_tiles + t])
-        inside = jnp.logical_and(place >= t * tile, place < (t + 1) * tile)
+        inside = jnp.logical_and(token >= t * tile, token < (t + 1) * tile)
         picked = jnp.where(inside, pick, picked)
     mine_before = picked > 0
 
@@ -250,6 +290,8 @@
             project(h - 1, pair[h - 1])
         sent(kv_copy, h, K)
         arrive(kv_copy, h, V)
+        if h == early - 1:
+            arrive(piece_copy)
         values = kv[V, :, :, columns(h)].reshape(3 * rows, HD)
         summed = jnp.dot(weights, values, preferred_element_type=jnp.float32)
         whole[...] = (summed / denominator).astype(jnp.bfloat16)
@@ -275,18 +317,51 @@
             merged.append(own + share[whose] * (other - own))
         return jnp.concatenate(merged, axis=0).T.astype(jnp.bfloat16)
 
+    def pass_on(copy_of, relays):
+        for way, there in relays:
+
+            @pl.when(there)
+            def _():
+                relay_on(way).wait_recv()
+                copy_of(way).start()
+
     for i in range(LATE):
         serve(i)
+        if i == 0:
+            pass_on(relay_on, near)
+            for h, which in queue[AT_ONCE:]:
+                if (h, which) == (early - 1, V):
+                    for way, there in joins:
+
+                        @pl.when(jnp.logical_and(ways[way][2], jnp.logical_not(there)))
+                        def _():
+                            piece_copy(way).start()
+
+                start(kv_copy, h, which)
     log_swap().start()
     for slot in (OWN, 1, 2):
         log_mid[slot, 0] = log_out[core, slot]
     for h in range(early):
         early_head(h)
         if h == 0:
+            for way, there in near:
+
+                @pl.when(there)
+                def _():
+                    relay_on(way).wait_send()
+
+            pass_on(relay_out, far)
             answer()
     att_swap(early - 1).wait()
     project(early - 1, pair[early - 1])
     log_swap().wait_send()
+    sent(piece_copy)
+    for way, there in far:
+
+        @pl.when(there)
+        def _():
+            relay_out(way).wait_send()
+
     for i in range(LATE):
         own_swap(i).wait()
         part_swap(i).wait_send()
@@ -355,6 +430,7 @@
             pltpu.VMEM((2, 3, LATE, 1, half), f32),
             pltpu.VMEM((3, 2, LATE, 1, half), f32),
             pltpu.VMEM((2, 2, LATE, 1, half), f32),
+            pltpu.VMEM((2, RELAYED, HD), bf16),
             pltpu.SMEM(kept[3].shape, jnp.int32),
             dma((4,)),
             dma((early * 4,)),
@@ -376,6 +452,10 @@
             dma((2,)),
             dma,
             dma,
+            dma((2,)),
+            dma((2,)),
+            dma((2,)),
+            dma((2,)),
         ],
         compiler_params=pltpu.CompilerParams(
             collective_id=0, has_side_effects=True, vmem_limit_bytes=48 << 20

time: 24.9 us -> 24.4 us (0.980)
  the two profiles are of different devices: /device:TPU:124 before, /device:TPU:1 now
where the time goes in v4:
time: 24.4 us; the launch traced here: 24 us
  Pallas kernels  24 us (98%)
    pallas_call x1, Pallas kernels, on_device(): pl.pallas_call(functools.partial(attend, heads), out_shape=(pltpu.VMEM((h...  22.8 us
    pallas_call x1, Pallas kernels, on_device(): pl.pallas_call(functools.partial(finish, blocks), out_shape=jax.ShapeDtyp...  1.16 us

profile of v4, /device:TPU:1, one launch (start us, length us, event | category | flops | bytes accessed | tf_op | source)
XLA Modules:
  0.0 24.0 jit_solution(15015902702608404223)
XLA Ops:
  0.0 22.8 %attend.1 = (f32[128,3072]{1,0:T(8,128)S(1)}, bf16[128,256]{1,0:T(8,128)(2,1)S(1)}, bf16[256,3072]{1,0:T(8,128)(2,1)S(1)}) custom-call(bf16[256,768]{1,0:T(8,128)(2,1)} %q_hbm.1, bf16[256,768]{1,0:T(8,128)(2,1)} %k_hbm.1, bf16[256,768]{1,0:T(8,128)(2,1)} %v_hbm.1, s32[8,128]{1,0:T(8,128)} %bitcast.1, bf16[768,3072]{1,0:T(8,128)(2,1)} %w_hbm.1), custom_call_target="tpu_custom_call" | custom-call | tf_op jit(solution)/shard_map/attend/pallas_call | solution.py:408
  22.8 1.2 %finish.1 = bf16[128,3072]{1,0:T(8,128)(2,1)} custom-call(f32[128,3072]{1,0:T(8,128)S(1)} %get-tuple-element.8.acc, bf16[128,256]{1,0:T(8,128)(2,1)S(1)} %get-tuple-element.9.att, bf16[256,3072]{1,0:T(8,128)(2,1)S(1)} %get-tuple-element.10.w), custom_call_target="tpu_custom_call" | custom-call | tf_op jit(solution)/shard_map/finish/pallas_call | solution.py:466

commit v5 on v4

--- a/solution.py
+++ b/solution.py
@@ -14,7 +14,7 @@
 K, V = 0, 1
 LATE = 3
 RING = 4
-AT_ONCE = 3
+AT_ONCE = 2
 RELAYED = 128
 
 
@@ -196,7 +196,8 @@
         start(kv_copy, h, which)
     for h in range(heads):
         w_mine(h).start()
-        w_swap(h).start()
+        if h < early:
+            w_swap(h).start()
     loads[3].wait()
 
     for slot, there in ((BEFORE, has_before), (AFTER, has_after)):
@@ -341,6 +342,9 @@
     log_swap().start()
     for slot in (OWN, 1, 2):
         log_mid[slot, 0] = log_out[core, slot]
+    answer()
+    for h in range(early, heads):
+        w_swap(h).start()
     for h in range(early):
         early_head(h)
         if h == 0:
@@ -351,7 +355,6 @@
                     relay_on(way).wait_send()
 
             pass_on(relay_out, far)
-            answer()
     att_swap(early - 1).wait()
     project(early - 1, pair[early - 1])
     log_swap().wait_send()

time: 24.4 us -> 24.4 us (level)
  no operation moved by 1% of the time
where the time goes in v5:
time: 24.4 us; the launch traced here: 24 us
  Pallas kernels  24 us (98%)
    pallas_call x1, Pallas kernels, on_device(): pl.pallas_call(functools.partial(attend, heads), out_shape=(pltpu.VMEM((h...  22.8 us
    pallas_call x1, Pallas kernels, on_device(): pl.pallas_call(functools.partial(finish, blocks), out_shape=jax.ShapeDtyp...  1.16 us

profile of v5, /device:TPU:1, one launch (start us, length us, event | category | flops | bytes accessed | tf_op | source)
XLA Modules:
  0.0 24.0 jit_solution(6470272968864073801)
XLA Ops:
  0.0 22.8 %attend.1 = (f32[128,3072]{1,0:T(8,128)S(1)}, bf16[128,256]{1,0:T(8,128)(2,1)S(1)}, bf16[256,3072]{1,0:T(8,128)(2,1)S(1)}) custom-call(bf16[256,768]{1,0:T(8,128)(2,1)} %q_hbm.1, bf16[256,768]{1,0:T(8,128)(2,1)} %k_hbm.1, bf16[256,768]{1,0:T(8,128)(2,1)} %v_hbm.1, s32[8,128]{1,0:T(8,128)} %bitcast.1, bf16[768,3072]{1,0:T(8,128)(2,1)} %w_hbm.1), custom_call_target="tpu_custom_call" | custom-call | tf_op jit(solution)/shard_map/attend/pallas_call | solution.py:411
  22.8 1.2 %finish.1 = bf16[128,3072]{1,0:T(8,128)(2,1)} custom-call(f32[128,3072]{1,0:T(8,128)S(1)} %get-tuple-element.8.acc, bf16[128,256]{1,0:T(8,128)(2,1)S(1)} %get-tuple-element.9.att, bf16[256,3072]{1,0:T(8,128)(2,1)S(1)} %get-tuple-element.10.w), custom_call_target="tpu_custom_call" | custom-call | tf_op jit(solution)/shard_map/finish/pallas_call | solution.py:469
